TPU v7x, 512 devices: a whole 4x4x16 slice. The times are simulated.
512 devices in a mesh: slab: 128 (over z, x, core), col: 4 (over y).
Axes of the slice: x: 4, y: 4, z: 16, core: 2. Of those that a mesh axis runs over, the one named last changes fastest.
Arguments:
- basis: bfloat16 [3, 64, 256, 32, 128], P(None, None, 'slab', 'col')
- cell_map: int32 [256, 32, 128], P('slab', 'col'), may hold values from 0 to 7
- table: float32 [8, 27], replicated, may hold values from 0 to 1, as said below
Outputs:
- next_block: bfloat16 [64, 256, 32, 128], P(None, 'slab', 'col')
- projections: float32 [2, 192, 64], replicated
- triangles: float32 [2, 64, 64], replicated
Inputs may be any that keep to these rules, and one draw needn't show every extreme that they name: `table`: coefficients lie between 0 and 1; the centre one is the largest.
All inputs are finite; a program needn't handle non-finite values.
Results may differ from a plain program's by a relative error of at most 0.027.
Values may be sent and summed in bfloat16 or wider, within the bound.
A program may use at most 64 MiB of HBM per device.

v0:
```python
import jax
import jax.numpy as jnp
from jax import lax
from jax.sharding import PartitionSpec as P


def extended(block, sides, width):
    for axis, dim in sides:
        count = lax.axis_size(axis)
        forward = [(i, i + 1) for i in range(count - 1)]
        backward = [(target, source) for source, target in forward]
        low = lax.ppermute(
            lax.slice_in_dim(block, block.shape[dim] - width, None, axis=dim), axis, forward
        )
        high = lax.ppermute(lax.slice_in_dim(block, 0, width, axis=dim), axis, backward)
        block = jnp.concatenate([low, block, high], axis=dim)
    return block


def apply_stencil(wide, coef):
    depth = wide.shape[3]
    rows_x = wide.shape[1] - 2
    rows_y = wide.shape[2] - 2
    padded = jnp.pad(wide, ((0, 0), (0, 0), (0, 0), (1, 1)))
    total = jnp.zeros((wide.shape[0], rows_x, rows_y, depth), jnp.float32)
    for dx in range(3):
        for dy in range(3):
            for dz in range(3):
                offset = 9 * dx + 3 * dy + dz
                piece = padded[:, dx : dx + rows_x, dy : dy + rows_y, dz : dz + depth].astype(
                    jnp.float32
                )
                total = total + coef[offset][None] * piece
    return total.astype(jnp.bfloat16)


def with_faces(block, coef):
    wide = extended(block, (("slab", 1), ("col", 2)), 1)
    return apply_stencil(wide, coef)


def lookup(cell_map, table):
    classes = table.shape[0]
    onehot = (cell_map[None] == jnp.arange(classes, dtype=jnp.int32)[:, None, None, None]).astype(
        jnp.float32
    )
    return jnp.einsum("ko,kxyz->oxyz", table, onehot, precision=lax.Precision.HIGHEST)


def gram_of(left, right, scale):
    return (
        lax.dot_general(left, right, (((1,), (1,)), ((), ())), preferred_element_type=jnp.float32)
        * scale
    )


def correct(stack, block, coeffs):
    moved = lax.dot_general(
        coeffs.astype(jnp.bfloat16),
        stack,
        (((0,), (0,)), ((), ())),
        preferred_element_type=jnp.float32,
    )
    return (block.astype(jnp.float32) - moved).astype(jnp.bfloat16)


def inner_part(flat, shape_wide):
    lead, span_x, span_y, depth = shape_wide
    cube = flat.reshape(lead, span_x, span_y, depth)
    return cube.reshape(lead, -1)


def orthonormalize(stack_wide, block_wide, shape_wide, scale):
    stack = inner_part(stack_wide, (stack_wide.shape[0],) + shape_wide[1:])
    block_inner = inner_part(block_wide, shape_wide)
    first = lax.psum(gram_of(stack, block_inner, 1.0), ("slab", "col")) * scale
    one_wide = correct(stack_wide, block_wide, first)
    second = (
        lax.psum(gram_of(stack, inner_part(one_wide, shape_wide), 1.0), ("slab", "col")) * scale
    )
    two_wide = correct(stack_wide, one_wide, second)
    two_inner = inner_part(two_wide, shape_wide)
    square = lax.psum(gram_of(two_inner, two_inner, 1.0), ("slab", "col")) * scale
    lower = jnp.linalg.cholesky(square)
    identity = jnp.eye(lower.shape[0], dtype=lower.dtype)
    inverse = lax.linalg.triangular_solve(lower, identity, left_side=True, lower=True)
    result = jnp.dot(
        inverse.astype(jnp.bfloat16), two_wide, preferred_element_type=jnp.float32
    ).astype(jnp.bfloat16)
    return (result, first + second, lower, None)


def shards(basis, cell_map, table):
    count_x, count_y, depth = cell_map.shape
    columns = basis.shape[1]
    devices_x = lax.axis_size("slab")
    devices_y = lax.axis_size("col")
    scale = 1.0 / (count_x * devices_x * count_y * devices_y * depth)
    coef = lookup(cell_map, table)
    flat = basis.reshape(3 * columns, count_x * count_y * depth)
    shape_inner = (columns, count_x, count_y, depth)
    image_first = with_faces(basis[2], coef)
    block_one, proj_one, lower_one, gram_one = orthonormalize(
        flat, image_first.reshape(columns, -1), shape_inner, scale
    )
    image = with_faces(block_one.reshape(shape_inner), coef)
    stack = jnp.concatenate([flat[columns:], block_one], axis=0)
    block_two, proj_two, lower_two, gram_two = orthonormalize(
        stack, image.reshape(columns, -1), shape_inner, scale
    )
    return (
        block_two.reshape(shape_inner),
        jnp.stack([proj_one, proj_two]),
        jnp.stack([lower_one, lower_two]),
    )


def solution(mesh):
    placed = (P(None, None, "slab", "col", None), P("slab", "col", None), P())
    return jax.shard_map(
        shards,
        mesh=mesh,
        in_specs=placed,
        out_specs=(P(None, "slab", "col", None), P(), P()),
        check_vma=False,
    )
```

profile of v0, /device:TPU:1, one launch (start us, length us, event | category | flops | bytes accessed | tf_op | source)
XLA Modules:
  0.0 697.7 jit_solution(16092930886953120736)
XLA Ops:
  1.7 4.5 collective-permute-start
  6.2 5.6 collective-permute-start.1
  13.2 2.7 collective-permute-start.2
  18.1 4.1 collective-permute-done.3
  22.2 2.8 fusion.11
  25.0 3.4 add_convert_fusion.1
  28.7 111.1 %psum.42 = f32[192,64]{0,1:T(8,128)S(1)} all-reduce(f32[192,64]{0,1:T(8,128)S(1)} %convolution_bitcast_fusion.2), channel_id=1, replica_groups=mesh['slab'=128,'col'=4] {'slab','col'}, use_global_device_ids=true, to_apply=%region_0.1 | all-reduce | flops 12288 | bytes 98304 | tf_op jit(solution)/shard_map/psum | solution.py:76
  140.5 99.1 %psum.43 = f32[192,64]{0,1:T(8,128)S(1)} all-reduce(f32[192,64]{0,1:T(8,128)S(1)} %convolution_bitcast_fusion.1), channel_id=1, replica_groups=mesh['slab'=128,'col'=4] {'slab','col'}, use_global_device_ids=true, to_apply=%region_1.2 | all-reduce | flops 12288 | bytes 98304 | tf_op jit(solution)/shard_map/psum | solution.py:79
  240.1 100.3 %psum.44 = f32[64,64]{0,1:T(8,128)S(1)} all-reduce(f32[64,64]{0,1:T(8,128)S(1)} %fusion.50), channel_id=1, replica_groups=mesh['slab'=128,'col'=4] {'slab','col'}, use_global_device_ids=true, to_apply=%region_2.3 | all-reduce | flops 4096 | bytes 32768 | tf_op jit(solution)/shard_map/psum | solution.py:83
  340.5 5.8 cholesky.44
  347.7 4.9 custom-call.6
  353.1 3.6 collective-permute-start.4
  357.0 1.9 collective-permute-start.5
  359.0 4.3 collective-permute-done.5
  363.5 1.3 collective-permute-start.6
  364.9 1.5 collective-permute-start.7
  366.8 4.0 collective-permute-done.7
  370.8 1.9 select_maximum_fusion
  372.7 3.3 add_convert_fusion
  376.4 105.5 %psum.45 = f32[192,64]{0,1:T(8,128)S(1)} all-reduce(f32[192,64]{0,1:T(8,128)S(1)} %fusion.15), channel_id=1, replica_groups=mesh['slab'=128,'col'=4] {'slab','col'}, use_global_device_ids=true, to_apply=%region_5.0 | all-reduce | flops 12288 | bytes 98304 | tf_op jit(solution)/shard_map/psum | solution.py:76
  482.6 99.5 %psum.46 = f32[192,64]{0,1:T(8,128)S(1)} all-reduce(f32[192,64]{0,1:T(8,128)S(1)} %fusion.44), channel_id=1, replica_groups=mesh['slab'=128,'col'=4] {'slab','col'}, use_global_device_ids=true, to_apply=%region_6.9 | all-reduce | flops 12288 | bytes 98304 | tf_op jit(solution)/shard_map/psum | solution.py:79
  582.6 100.3 %psum.47 = f32[64,64]{0,1:T(8,128)S(1)} all-reduce(f32[64,64]{0,1:T(8,128)S(1)} %fusion.51), channel_id=1, replica_groups=mesh['slab'=128,'col'=4] {'slab','col'}, use_global_device_ids=true, to_apply=%region_7.10 | all-reduce | flops 4096 | bytes 32768 | tf_op jit(solution)/shard_map/psum | solution.py:83
  683.0 5.8 cholesky.55
  690.2 4.9 custom-call.7
  (57 shorter events, 14.3 us)
Async XLA Ops:
  0.6 11.2 %copy-start = (f32[8,27]{1,0:T(8,128)S(1)}, f32[8,27]{1,0:T(8,128)}, u32[]{:S(2)}) copy-start(f32[8,27]{1,0:T(8,128)} %param.8) | copy-start | bytes 2596
  0.6 16.7 %copy-start.1 = (bf16[3,64,2,8,128]{4,3,2,1,0:T(8,128)(2,1)S(1)}, bf16[3,64,2,8,128]{4,3,2,1,0:T(8,128)(2,1)}, u32[]{:S(2)}) copy-start(bf16[3,64,2,8,128]{4,3,2,1,0:T(8,128)(2,1)} %param.6) | copy-start | bytes 2359300
  1.7 11.2 %collective-permute-start = (bf16[64,1,8,128]{3,2,1,0:T(8,128)(2,1)S(1)}, bf16[64,1,8,128]{3,2,1,0:T(8,128)(2,1)S(1)}, u32[]{:S(2)}, u32[]{:S(2)}) collective-permute-start(bf16[64,1,8,128]{3,2,1,0:T(8,128)(2,1)S(1)} %get-tuple-element.38), channel_id=1, source_target_pairs={{0,4},{4,8},{8,12},{12,16},{16,20},{20,24},{24,28},{28,32},{32,36}... | collective-permute-start | bytes 393224 | tf_op jit(solution)/shard_map/ppermute | solution.py:12
  6.2 6.7 collective-permute-start.1
  13.2 4.9 collective-permute-start.2
  15.9 6.3 collective-permute-start.3
  239.8 116.9 %slice-start = ((bf16[3,64,2,8,128]{4,3,2,1,0:T(8,128)(2,1)}), bf16[2,64,2,8,128]{4,3,2,1,0:T(8,128)(2,1)S(1)}, s32[]{:S(2)}) async-start(bf16[3,64,2,8,128]{4,3,2,1,0:T(8,128)(2,1)} %param.6), calls=%async_computation | async-start | bytes 1048576 | tf_op jit(solution)/shard_map/slice | solution.py:107
  353.1 5.8 collective-permute-start.4
  357.0 6.3 collective-permute-start.5
  363.5 3.3 collective-permute-start.6
  364.9 5.9 collective-permute-start.7
where the time goes:
time: 699 us; the launch traced here: 698 us
  blocking collectives  616 us (88%)
  other arithmetic  37 us (5%)
  starting transfers between devices  22.5 us (3%)
  waiting for transfers between devices  13.3 us (2%)
    psum x2, blocking collectives, orthonormalize(): first = lax.psum(gram_of(stack, block_inner, 1.0), ('slab', 'col')) * scale  217 us
    psum x2, blocking collectives, orthonormalize(): lax.psum(gram_of(two_inner, two_inner, 1.0), ('slab', 'col')) * scale  201 us
    psum x2, blocking collectives, orthonormalize(): lax.psum(gram_of(stack, inner_part(one_wide, shape_wide), 1.0), ('slab',...  199 us
  transfers between devices with their start and end apart: 8, of which 5 were waited for; matrix products, arithmetic and copies ran while one was open for 0% of the time, Pallas kernels for 0%

commit v1 on v0

--- a/solution.py
+++ b/solution.py
@@ -80,7 +80,9 @@
     )
     two_wide = correct(stack_wide, one_wide, second)
     two_inner = inner_part(two_wide, shape_wide)
-    square = lax.psum(gram_of(two_inner, two_inner, 1.0), ("slab", "col")) * scale
+    square = (
+        jnp.sum(lax.all_gather(gram_of(two_inner, two_inner, 1.0), ("slab", "col")), axis=0) * scale
+    )
     lower = jnp.linalg.cholesky(square)
     identity = jnp.eye(lower.shape[0], dtype=lower.dtype)
     inverse = lax.linalg.triangular_solve(lower, identity, left_side=True, lower=True)

time: 699 us -> 956 us (1.37)
  waiting for transfers between devices: 13.3 us -> 443 us
  blocking collectives: 616 us -> 415 us
  other arithmetic: 37 us -> 50.9 us
  between operations: 1.04 us -> 14.4 us
    all_gather x0 -> x2, waiting for transfers between devices: none -> 430 us  [orthonormalize(): lax.all_gather(gram_of(two_inner, two_inner, 1.0), ('slab', 'col'))]
    psum x2 -> x0, blocking collectives: 201 us -> none  [orthonormalize(): lax.psum(gram_of(two_inner, two_inner, 1.0), ('slab', 'col')) * scale]
    reduce_sum x0 -> x2, other arithmetic: none -> 13.9 us  [orthonormalize(): jnp.sum(lax.all_gather(gram_of(two_inner, two_inner, 1.0), ('slab', 'col'...]
  transfers between devices with their start and end apart: 8 -> 10, of which waited for: 5 -> 7; matrix products, arithmetic and copies ran while one was open for 0% -> 0% of each run, Pallas kernels for 0% -> 0%
where the time goes in v1:
time: 956 us; the launch traced here: 955 us
  waiting for transfers between devices  443 us (46%)
  blocking collectives  415 us (43%)
  other arithmetic  50.9 us (5%)
  starting transfers between devices  22.6 us (2%)
  between operations  14.4 us (2%)
    all_gather x2, waiting for transfers between devices, orthonormalize(): lax.all_gather(gram_of(two_inner, two_inner, 1.0), ('slab', 'col'))  430 us
    psum x2, blocking collectives, orthonormalize(): first = lax.psum(gram_of(stack, block_inner, 1.0), ('slab', 'col')) * scale  217 us
    psum x2, blocking collectives, orthonormalize(): lax.psum(gram_of(stack, inner_part(one_wide, shape_wide), 1.0), ('slab',...  198 us
  transfers between devices with their start and end apart: 10, of which 7 were waited for; matrix products, arithmetic and copies ran while one was open for 0% of the time, Pallas kernels for 0%

profile of v1, /device:TPU:1, one launch (start us, length us, event | category | flops | bytes accessed | tf_op | source)
XLA Modules:
  0.0 954.9 jit_solution(7426203617737928314)
XLA Ops:
  8.3 4.5 collective-permute-start
  12.8 5.6 collective-permute-start.1
  19.8 2.8 collective-permute-start.2
  24.7 4.1 collective-permute-done.3
  28.8 2.8 fusion.11
  31.6 3.4 add_convert_fusion.1
  35.3 111.1 %psum.28 = f32[192,64]{0,1:T(8,128)S(1)} all-reduce(f32[192,64]{0,1:T(8,128)S(1)} %convolution_bitcast_fusion.2), channel_id=1, replica_groups=mesh['slab'=128,'col'=4] {'slab','col'}, use_global_device_ids=true, to_apply=%region_0.1 | all-reduce | flops 12288 | bytes 98304 | tf_op jit(solution)/shard_map/psum | solution.py:76
  147.1 99.1 %psum.29 = f32[192,64]{0,1:T(8,128)S(1)} all-reduce(f32[192,64]{0,1:T(8,128)S(1)} %convolution_bitcast_fusion.1), channel_id=1, replica_groups=mesh['slab'=128,'col'=4] {'slab','col'}, use_global_device_ids=true, to_apply=%region_1.2 | all-reduce | flops 12288 | bytes 98304 | tf_op jit(solution)/shard_map/psum | solution.py:79
  247.3 215.3 %all-gather.5.cloned.1.call-done = f32[32768,64]{1,0:T(8,128)} async-done(((f32[64,64]{1,0:T(8,128)}), f32[32768,64]{1,0:T(8,128)}) %all-gather.5.cloned.1.call-update) | async-done | bytes 8388624 | tf_op jit(solution)/shard_map/all_gather | solution.py:84
  462.6 6.9 reduce_sum.18
  469.8 5.8 cholesky.44
  477.0 4.9 custom-call.6
  482.4 2.4 collective-permute-start.4
  484.9 1.9 collective-permute-start.5
  486.9 4.3 collective-permute-done.5
  491.4 2.6 collective-permute-start.6
  495.9 3.8 collective-permute-done.7
  501.6 3.3 add_convert_fusion
  505.3 105.4 %psum.30 = f32[192,64]{0,1:T(8,128)S(1)} all-reduce(f32[192,64]{0,1:T(8,128)S(1)} %fusion.15), channel_id=1, replica_groups=mesh['slab'=128,'col'=4] {'slab','col'}, use_global_device_ids=true, to_apply=%region_5.0 | all-reduce | flops 12288 | bytes 98304 | tf_op jit(solution)/shard_map/psum | solution.py:76
  611.4 99.0 %psum.31 = f32[192,64]{0,1:T(8,128)S(1)} all-reduce(f32[192,64]{0,1:T(8,128)S(1)} %fusion.44), channel_id=1, replica_groups=mesh['slab'=128,'col'=4] {'slab','col'}, use_global_device_ids=true, to_apply=%region_6.9 | all-reduce | flops 12288 | bytes 98304 | tf_op jit(solution)/shard_map/psum | solution.py:79
  712.3 214.7 %all-gather.7.cloned.1.call-done = f32[32768,64]{1,0:T(8,128)} async-done(((f32[64,64]{1,0:T(8,128)}), f32[32768,64]{1,0:T(8,128)}) %all-gather.7.cloned.1.call-update) | async-done | bytes 8388624 | tf_op jit(solution)/shard_map/all_gather | solution.py:84
  927.0 6.9 reduce_sum.19
  934.1 5.8 cholesky.55
  941.3 4.9 custom-call.7
  (65 shorter events, 19.0 us)
Async XLA Ops:
  7.2 11.2 %copy-start = (f32[8,27]{1,0:T(8,128)S(1)}, f32[8,27]{1,0:T(8,128)}, u32[]{:S(2)}) copy-start(f32[8,27]{1,0:T(8,128)} %param.8) | copy-start | bytes 2596
  7.2 16.7 %copy-start.1 = (bf16[3,64,2,8,128]{4,3,2,1,0:T(8,128)(2,1)S(1)}, bf16[3,64,2,8,128]{4,3,2,1,0:T(8,128)(2,1)}, u32[]{:S(2)}) copy-start(bf16[3,64,2,8,128]{4,3,2,1,0:T(8,128)(2,1)} %param.6) | copy-start | bytes 2359300
  7.2 455.5 %all-gather.5.cloned.1.call-start = ((), (), s32[]{:S(2)}) async-start(), calls=%async_computation | async-start | bytes 16809984 | tf_op jit(solution)/shard_map/all_gather | solution.py:84
  8.3 11.2 %collective-permute-start = (bf16[64,1,8,128]{3,2,1,0:T(8,128)(2,1)S(1)}, bf16[64,1,8,128]{3,2,1,0:T(8,128)(2,1)S(1)}, u32[]{:S(2)}, u32[]{:S(2)}) collective-permute-start(bf16[64,1,8,128]{3,2,1,0:T(8,128)(2,1)S(1)} %get-tuple-element.38), channel_id=1, source_target_pairs={{0,4},{4,8},{8,12},{12,16},{16,20},{20,24},{24,28},{28,32},{32,36}... | collective-permute-start | bytes 393224 | tf_op jit(solution)/shard_map/ppermute | solution.py:12
  12.8 6.7 collective-permute-start.1
  19.8 4.9 collective-permute-start.2
  22.5 6.3 collective-permute-start.3
  247.3 679.7 %all-gather.7.cloned.1.call-start = ((), (), s32[]{:S(2)}) async-start(), calls=%async_computation.1 | async-start | bytes 16809984 | tf_op jit(solution)/shard_map/all_gather | solution.py:84
  482.1 13.3 %slice-start = ((bf16[3,64,2,8,128]{4,3,2,1,0:T(8,128)(2,1)}), bf16[2,64,2,8,128]{4,3,2,1,0:T(8,128)(2,1)S(1)}, s32[]{:S(2)}) async-start(bf16[3,64,2,8,128]{4,3,2,1,0:T(8,128)(2,1)} %param.6), calls=%async_computation.2 | async-start | bytes 1048576 | tf_op jit(solution)/shard_map/slice | solution.py:109
  482.4 4.4 collective-permute-start.4
  484.9 6.3 collective-permute-start.5
  491.4 4.5 collective-permute-start.6
  494.0 5.7 collective-permute-start.7
Sparse Core Ops, SparseCore 0:
  247.4 215.2 all-gather.4
  711.7 215.2 all-gather.6
